TPU v7x, 32 devices: a whole 2x2x4 slice. The times are simulated.
32 devices in a mesh: period: 16 (over z, y, x), half: 2 (over core).
Axes of the slice: x: 2, y: 2, z: 4, core: 2. Of those that a mesh axis runs over, the one named last changes fastest.
Arguments:
- probes: float32 [128, 4, 512], P('period', None, 'half'), may hold values from -6 to 6
- footprints: bfloat16 [128, 512, 512], P('period', None, 'half'), may hold values from -0.25 to 0.25
- lag_weights: float32 [128, 4], P('period'), may hold values from 0.2 to 2
- owners: int32 [128, 4], P('period'), may hold values from 0 to 15, all different within a row; in each aligned block of 8 rows (0 to 7, 8 to 15, ...) at most 4 rows name the same one
- window_tiles: int32 [128, 2], P('period', 'half'), may hold values from 0 to 10
- coords: int32 [2, 3072], replicated, may hold values from 0 to 63
- temporal: float32 [16, 16], replicated, as said below
Outputs:
- coefficients: float32 [4, 4], replicated
- residual: float32 [128, 4, 512], P('period', None, 'half')
Inputs may be any that keep to these rules, and one draw needn't show every extreme that they name: `owners`: each row names 4 different periods. Among the 8 rows of one index of period, no period is named more than 4 times, and one is named exactly 4 times. `temporal`: symmetric.
All inputs are finite; a program needn't handle non-finite values.
Results may differ from a plain program's by a relative error of at most 0.025.
Values may be sent and summed in bfloat16 or wider, within the bound.
A program may use at most 64 MiB of HBM per device.

v0:
```python
import jax
import jax.numpy as jnp
from jax import lax
from jax.sharding import PartitionSpec as P

epsilon = 1e-06
kernel_scale = 0.05
kernel_length = 6.0
highest = lax.Precision.HIGHEST


def from_partner(block, axis, bit):
    count = lax.axis_size(axis)
    route = []
    for low in range(count):
        high = low | 1 << bit
        if high != low and high < count:
            route += [(low, high), (high, low)]
    return lax.ppermute(block, axis, route)


def body(probes, footprints, lag_weights, owners, window_tiles, coords, temporal):
    periods = lax.axis_size("period")
    half_index = lax.axis_index("half")
    block_count, top_count = owners.shape
    probe_count = probes.shape[1]
    sound_count = footprints.shape[1]
    window = footprints.shape[2]
    win_tiles = window // 128
    cell_count = coords.shape[1]
    half_cells = cell_count // 2
    tile_count = half_cells // 128
    group_cells = half_cells // periods
    capacity = max(2, 2 * block_count * top_count // periods)
    pair_count = block_count * top_count
    slot_count = periods * capacity
    total_rows = float(block_count * periods * sound_count)
    tiles = window_tiles[:, 0]
    own_coords = lax.dynamic_slice_in_dim(coords, half_index * half_cells, half_cells, 1)
    delta_x = own_coords[0][:, None] - coords[0][None, :]
    delta_y = own_coords[1][:, None] - coords[1][None, :]
    squared = (delta_x * delta_x + delta_y * delta_y).astype(jnp.float32)
    kernel_rows = (kernel_scale * jnp.exp(-jnp.sqrt(squared) / kernel_length)).reshape(
        periods, group_cells, cell_count
    )
    destination = owners.reshape(pair_count)
    pair_index = jnp.arange(pair_count, dtype=jnp.int32)
    earlier = (destination[None, :] == destination[:, None]) & (
        pair_index[None, :] < pair_index[:, None]
    )
    slot_rank = jnp.sum(earlier.astype(jnp.int32), axis=1)
    slot_index = destination * capacity + slot_rank
    slot_hot_int = (slot_index[None, :] == jnp.arange(slot_count, dtype=jnp.int32)[:, None]).astype(
        jnp.int32
    )
    slot_hot = slot_hot_int.astype(jnp.float32)
    pair_tiles = jnp.repeat(tiles, top_count)
    wanted = jnp.sum(slot_hot_int * pair_tiles[None, :], axis=1).reshape(periods, capacity)
    asked = lax.all_to_all(wanted, "period", split_axis=0, concat_axis=0, tiled=True)
    asked_hot = (
        asked[:, :, None, None] + jnp.arange(win_tiles, dtype=jnp.int32)[None, None, :, None]
        == jnp.arange(tile_count, dtype=jnp.int32)[None, None, None, :]
    ).astype(jnp.float32)

    def add_half(piece_rows):
        return jnp.einsum(
            "bps,bsw->bpw", piece_rows, footprints, preferred_element_type=jnp.float32
        )

    def mix_periods(grouped_part):
        mixed_part = jnp.einsum("ts,sik->tik", temporal, grouped_part, precision=highest)
        return lax.all_to_all(mixed_part, "period", split_axis=0, concat_axis=0, tiled=True)

    def apply_operator(vector):
        vector_low = vector.astype(jnp.bfloat16)
        partial_value = add_half(lax.all_gather(vector_low, "half", axis=2, tiled=True))
        terms = lag_weights[:, :, None, None] * partial_value[:, None, :, :]
        outgoing = jnp.dot(
            slot_hot, terms.reshape(pair_count, probe_count * window), precision=highest
        )
        outgoing = outgoing.reshape(periods, capacity, probe_count, win_tiles, 128)
        received = lax.all_to_all(
            outgoing.astype(jnp.bfloat16), "period", split_axis=0, concat_axis=0, tiled=True
        ).astype(outgoing.dtype)
        flux_half = jnp.einsum("ncpjl,ncjt->ptl", received, asked_hot, precision=highest).reshape(
            probe_count, half_cells
        )
        other_half = from_partner(flux_half, "half", 0)
        whole_flux = jnp.where(
            half_index == 0,
            jnp.concatenate([flux_half, other_half], axis=1),
            jnp.concatenate([other_half, flux_half], axis=1),
        )
        grouped = jnp.einsum("pc,gkc->gpk", whole_flux, kernel_rows, precision=highest)
        mixed_flux = mix_periods(
            lax.all_to_all(grouped, "period", split_axis=0, concat_axis=0, tiled=True)
        )
        field_low = (
            jnp.transpose(mixed_flux, (1, 0, 2))
            .reshape(probe_count, half_cells)
            .astype(jnp.bfloat16)
        )
        field_tiles = field_low.reshape(probe_count, tile_count, 128)
        answers = jnp.einsum(
            "ptl,ncjt->ncpjl",
            field_tiles,
            asked_hot.astype(jnp.bfloat16),
            preferred_element_type=jnp.float32,
        )
        answers = answers.astype(jnp.bfloat16)
        returned = lax.all_to_all(answers, "period", split_axis=0, concat_axis=0, tiled=True)
        windows = jnp.dot(
            slot_hot.astype(jnp.bfloat16).T,
            returned.reshape(slot_count, probe_count * window),
            preferred_element_type=jnp.float32,
        )
        windows = windows.astype(jnp.bfloat16).reshape(block_count, top_count, probe_count, window)
        products = jnp.einsum(
            "bkpw,bsw->bkps", windows, footprints, preferred_element_type=jnp.float32
        )
        sounded = jnp.einsum("bk,bkps->bps", lag_weights, products, precision=highest)
        return lax.psum_scatter(
            sounded.astype(jnp.bfloat16), "half", scatter_dimension=2, tiled=True
        ).astype(jnp.float32)

    def local_mean(values):
        return jnp.sum(values, axis=(0, 2))

    def lanczos_step(current, image):
        inner_sum = lax.psum(local_mean(current * image), ("period", "half"))
        alpha = inner_sum / total_rows
        remainder = image - alpha[None, :, None] * current
        square_sum = lax.psum(local_mean(remainder * remainder), ("period", "half"))
        beta = jnp.sqrt(square_sum / total_rows + epsilon)
        return (alpha, remainder, beta)

    start_sum = lax.psum(local_mean(probes * probes), ("period", "half"))
    first_q = probes / jnp.sqrt(start_sum / total_rows + epsilon)[None, :, None]
    image_one = apply_operator(first_q)
    alpha_one, rest_one, beta_one = lanczos_step(first_q, image_one)
    second_q = rest_one / beta_one[None, :, None]
    image_two = apply_operator(second_q) - beta_one[None, :, None] * first_q
    alpha_two, residual, beta_two = lanczos_step(second_q, image_two)
    coefficients = jnp.stack([alpha_one, beta_one, alpha_two, beta_two], axis=0)
    return (coefficients, residual)


def solution(mesh):
    in_specs = (
        P("period", None, "half"),
        P("period", None, "half"),
        P("period", None),
        P("period", None),
        P("period", "half"),
        P(),
        P(),
    )
    out_specs = (P(), P("period", None, "half"))
    return jax.shard_map(body, mesh=mesh, in_specs=in_specs, out_specs=out_specs, check_vma=False)
```

profile of v0, /device:TPU:0, one launch (start us, length us, event | category | flops | bytes accessed | tf_op | source)
XLA Modules:
  0.0 438.8 jit_solution(13188646093719657682)
XLA Ops:
  10.0 8.3 %all-to-all-start = ((s32[16,1,4]{2,1,0:T(1,128)}), s32[16,1,4]{2,1,0:T(1,128)S(1)}, u32[]{:S(2)}, u32[]{:S(2)}) async-start(s32[16,1,4]{2,1,0:T(1,128)} %bitcast.1), calls=%async_computation | async-start | bytes 16384 | tf_op jit(solution)/shard_map/all_to_all | solution.py:59
  19.2 40.7 %psum.35 = f32[4]{0:T(128)S(1)} all-reduce(f32[4]{0:T(128)S(1)} %multiply_reduce_fusion.3), channel_id=1, replica_groups=mesh['period'=16,'half'=2] {'period','half'}, use_global_device_ids=true, to_apply=%region_1.0 | all-reduce | flops 4 | bytes 32 | tf_op jit(solution)/shard_map/psum | solution.py:137
  61.6 1.8 all_gather.6
  65.2 5.4 %all-to-all-start.1 = ((bf16[16,4,4,2,128]{4,3,1,2,0:T(2,128)(2,1)}), bf16[16,4,4,2,128]{4,3,1,2,0:T(2,128)(2,1)S(1)}, u32[]{:S(2)}, u32[]{:S(2)}) async-start(bf16[16,4,4,2,128]{4,3,1,2,0:T(2,128)(2,1)} %copy.68), calls=%async_computation.1 | async-start | bytes 262144 | tf_op jit(solution)/shard_map/all_to_all | solution.py:82
  70.7 7.7 %all-to-all-done.1 = bf16[16,4,4,2,128]{4,3,1,2,0:T(2,128)(2,1)S(1)} async-done(((bf16[16,4,4,2,128]{4,3,1,2,0:T(2,128)(2,1)}), bf16[16,4,4,2,128]{4,3,1,2,0:T(2,128)(2,1)S(1)}, u32[]{:S(2)}, u32[]{:S(2)}) %all-to-all-start.1) | async-done | bytes 131104 | tf_op jit(solution)/shard_map/all_to_all | solution.py:82
  80.0 43.0 %fusion.20 = f32[16,4,96]{2,1,0:T(4,128)S(1)} fusion(s32[3072]{0:T(1024)S(1)} %bitcast.152, s32[16,96]{1,0:T(8,128)S(1)} %sub.50, s32[3072]{0:T(1024)S(1)} %bitcast.150, s32[16,96]{1,0:T(8,128)S(1)} %sub.45, f32[4,1536]{1,0:T(4,128)S(1)} %collective-permute-done, f32[4,1536]{1,0:T(4,128)S(1)} %bitcast.147, pred[]{:T(512)S(6)} %eq.71), kind=kOutput, calls=%fused_computation.27 | convolution fusion | flops 268996608 | bytes 110593 | tf_op jit(solution)/shard_map/pc,gkc->gpk/dot_general | solution.py:94
  123.0 10.3 %all_to_all.49 = f32[16,4,96]{2,1,0:T(4,128)S(1)} all-to-all(f32[16,4,96]{2,1,0:T(4,128)S(1)} %fusion.20), channel_id=1, replica_groups=mesh['period'=16,'half'=2] {'period'}, dimensions={0} | all-to-all | bytes 49152 | tf_op jit(solution)/shard_map/all_to_all | solution.py:96
  133.5 9.9 %all_to_all.50 = bf16[16,4,96]{2,1,0:T(4,128)(2,1)S(1)} all-to-all(bf16[16,4,96]{2,1,0:T(4,128)(2,1)S(1)} %copy.72), channel_id=1, replica_groups=mesh['period'=16,'half'=2] {'period'}, dimensions={0} | all-to-all | bytes 24576 | tf_op jit(solution)/shard_map/all_to_all | solution.py:72
  144.4 3.5 all-to-all-start.4
  148.1 7.6 %all-to-all-done.4 = bf16[16,4,4,2,128]{4,2,3,1,0:T(4,128)(2,1)S(1)} async-done(((bf16[16,4,4,2,128]{4,2,3,1,0:T(4,128)(2,1)}), bf16[16,4,4,2,128]{4,2,3,1,0:T(4,128)(2,1)S(1)}, u32[]{:S(2)}, u32[]{:S(2)}) %all-to-all-start.4) | async-done | bytes 131104 | tf_op jit(solution)/shard_map/all_to_all | solution.py:111
  158.2 1.3 reshape.155
  159.5 4.8 %reduce-scatter.7.cloned.1.call-done = bf16[256,32]{1,0:T(8,128)(2,1)} async-done(((bf16[512,32]{1,0:T(8,128)(2,1)}), bf16[256,32]{1,0:T(8,128)(2,1)}) %reduce-scatter.7.cloned.1.call-update) | async-done | bytes 16400
  166.0 40.5 %psum.36 = f32[4]{0:T(128)S(1)} all-reduce(f32[4]{0:T(128)S(1)} %fusion.47), channel_id=1, replica_groups=mesh['period'=16,'half'=2] {'period','half'}, use_global_device_ids=true, to_apply=%region_6.7 | all-reduce | flops 4 | bytes 32 | tf_op jit(solution)/shard_map/psum | solution.py:130
  206.7 40.0 %psum.37 = f32[4]{0:T(128)S(1)} all-reduce(f32[4]{0:T(128)S(1)} %multiply_reduce_fusion.2), channel_id=1, replica_groups=mesh['period'=16,'half'=2] {'period','half'}, use_global_device_ids=true, to_apply=%region_8.9 | all-reduce | flops 4 | bytes 32 | tf_op jit(solution)/shard_map/psum | solution.py:133
  246.9 1.8 all_gather.7
  249.9 14.0 %all_to_all.51 = bf16[16,4,4,2,128]{4,3,1,2,0:T(2,128)(2,1)S(1)} all-to-all(bf16[16,4,4,2,128]{4,3,1,2,0:T(2,128)(2,1)S(1)} %copy.77), channel_id=1, replica_groups=mesh['period'=16,'half'=2] {'period'}, dimensions={0} | all-to-all | bytes 262144 | tf_op jit(solution)/shard_map/all_to_all | solution.py:82
  265.4 43.0 %fusion.21 = f32[16,4,96]{2,1,0:T(4,128)S(1)} fusion(s32[3072]{0:T(1024)S(1)} %bitcast.153, s32[16,96]{1,0:T(8,128)S(1)} %sub.50, s32[3072]{0:T(1024)S(1)} %bitcast.151, s32[16,96]{1,0:T(8,128)S(1)} %sub.45, f32[4,1536]{1,0:T(4,128)S(1)} %collective-permute-done.1, f32[4,1536]{1,0:T(4,128)S(1)} %bitcast.149, pred[]{:T(512)S(6)} %eq.71), kind=kOutput, calls=%fused_computation.28 | convolution fusion | flops 268996608 | bytes 110593 | tf_op jit(solution)/shard_map/pc,gkc->gpk/dot_general | solution.py:94
  308.3 10.3 %all_to_all.52 = f32[16,4,96]{2,1,0:T(4,128)S(1)} all-to-all(f32[16,4,96]{2,1,0:T(4,128)S(1)} %fusion.21), channel_id=1, replica_groups=mesh['period'=16,'half'=2] {'period'}, dimensions={0} | all-to-all | bytes 49152 | tf_op jit(solution)/shard_map/all_to_all | solution.py:96
  318.9 9.9 %all_to_all.53 = bf16[16,4,96]{2,1,0:T(4,128)(2,1)S(1)} all-to-all(bf16[16,4,96]{2,1,0:T(4,128)(2,1)S(1)} %copy.81), channel_id=1, replica_groups=mesh['period'=16,'half'=2] {'period'}, dimensions={0} | all-to-all | bytes 24576 | tf_op jit(solution)/shard_map/all_to_all | solution.py:72
  329.2 10.4 %all_to_all.54 = bf16[16,4,4,2,128]{4,2,3,1,0:T(4,128)(2,1)S(1)} all-to-all(bf16[16,4,4,2,128]{4,2,3,1,0:T(4,128)(2,1)S(1)} %copy.83), channel_id=1, replica_groups=mesh['period'=16,'half'=2] {'period'}, dimensions={0} | all-to-all | bytes 262144 | tf_op jit(solution)/shard_map/all_to_all | solution.py:111
  342.0 1.3 reshape.157
  343.4 4.8 %reduce-scatter.9.cloned.1.call-done = bf16[256,32]{1,0:T(8,128)(2,1)} async-done(((bf16[512,32]{1,0:T(8,128)(2,1)}), bf16[256,32]{1,0:T(8,128)(2,1)}) %reduce-scatter.9.cloned.1.call-update) | async-done | bytes 16400
  349.9 40.5 %psum.38 = f32[4]{0:T(128)S(1)} all-reduce(f32[4]{0:T(128)S(1)} %multiply_reduce_fusion.1), channel_id=1, replica_groups=mesh['period'=16,'half'=2] {'period','half'}, use_global_device_ids=true, to_apply=%region_11.12 | all-reduce | flops 4 | bytes 32 | tf_op jit(solution)/shard_map/psum | solution.py:130
  391.3 40.0 %psum.39 = f32[4]{0:T(128)S(1)} all-reduce(f32[4]{0:T(128)S(1)} %get-tuple-element.4), channel_id=1, replica_groups=mesh['period'=16,'half'=2] {'period','half'}, use_global_device_ids=true, to_apply=%region_13.14 | all-reduce | flops 4 | bytes 32 | tf_op jit(solution)/shard_map/psum | solution.py:133
  (98 shorter events, 23.3 us)
Async XLA Ops:
  7.2 56.2 %copy-start = (bf16[8,512,256]{2,1,0:T(8,128)(2,1)S(1)}, bf16[8,512,256]{2,1,0:T(8,128)(2,1)}, u32[]{:S(2)}) copy-start(bf16[8,512,256]{2,1,0:T(8,128)(2,1)} %param.8) | copy-start | bytes 6291460
  10.0 55.3 %all-to-all-start = ((s32[16,1,4]{2,1,0:T(1,128)}), s32[16,1,4]{2,1,0:T(1,128)S(1)}, u32[]{:S(2)}, u32[]{:S(2)}) async-start(s32[16,1,4]{2,1,0:T(1,128)} %bitcast.1), calls=%async_computation | async-start | bytes 16384 | tf_op jit(solution)/shard_map/all_to_all | solution.py:59
  63.4 15.4 %copy-start.1 = (s32[2,3072]{1,0:T(2,128)S(1)}, s32[2,3072]{1,0:T(2,128)}, u32[]{:S(2)}) copy-start(s32[2,3072]{1,0:T(2,128)} %param.12) | copy-start | bytes 73732
  65.2 13.2 %all-to-all-start.1 = ((bf16[16,4,4,2,128]{4,3,1,2,0:T(2,128)(2,1)}), bf16[16,4,4,2,128]{4,3,1,2,0:T(2,128)(2,1)S(1)}, u32[]{:S(2)}, u32[]{:S(2)}) async-start(bf16[16,4,4,2,128]{4,3,1,2,0:T(2,128)(2,1)} %copy.68), calls=%async_computation.1 | async-start | bytes 262144 | tf_op jit(solution)/shard_map/all_to_all | solution.py:82
  78.7 1.3 collective-permute-start
  80.0 53.3 %copy-start.2 = (f32[16,16]{1,0:T(8,128)S(1)}, f32[16,16]{1,0:T(8,128)}, u32[]{:S(2)}) copy-start(f32[16,16]{1,0:T(8,128)} %param.13) | copy-start | bytes 3076
  80.0 68.0 %copy-start.3 = (f32[8,4]{0,1:T(4,128)S(1)}, f32[8,4]{0,1:T(4,128)}, u32[]{:S(2)}) copy-start(f32[8,4]{0,1:T(4,128)} %param.9) | copy-start | bytes 388
  144.4 11.3 %all-to-all-start.4 = ((bf16[16,4,4,2,128]{4,2,3,1,0:T(4,128)(2,1)}), bf16[16,4,4,2,128]{4,2,3,1,0:T(4,128)(2,1)S(1)}, u32[]{:S(2)}, u32[]{:S(2)}) async-start(bf16[16,4,4,2,128]{4,2,3,1,0:T(4,128)(2,1)} %copy.74), calls=%async_computation.4 | async-start | bytes 262144 | tf_op jit(solution)/shard_map/all_to_all | solution.py:111
  147.9 16.4 %reduce-scatter.7.cloned.1.call-start = ((), (), s32[]{:S(2)}) async-start(), calls=%async_computation.11 | async-start | bytes 196608
  159.5 188.7 %reduce-scatter.9.cloned.1.call-start = ((), (), s32[]{:S(2)}) async-start(), calls=%async_computation.12 | async-start | bytes 196608
  264.1 1.3 collective-permute-start.1
Sparse Core Ops, SparseCore 0:
  159.6 4.6 reduce-scatter.6
  343.5 4.6 reduce-scatter.8
where the time goes:
time: 440 us; the launch traced here: 439 us
  blocking collectives  270 us (61%)
  matrix products  91.7 us (21%)
  waiting for transfers between devices  27 us (6%)
  starting transfers between devices  17.5 us (4%)
  between operations  14.4 us (3%)
  local copies, waits for them, and re-layouts  13.6 us (3%)
    dot_general x2, matrix products, apply_operator(): jnp.einsum('pc,gkc->gpk', whole_flux, kernel_rows, precision=highest)  85.9 us
    psum x2, blocking collectives, lanczos_step(): inner_sum = lax.psum(local_mean(current * image), ('period', 'half'))  81.1 us
    psum x2, blocking collectives, lanczos_step(): square_sum = lax.psum(local_mean(remainder * remainder), ('period', 'half'))  80.1 us
    psum x1, blocking collectives, body(): start_sum = lax.psum(local_mean(probes * probes), ('period', 'half'))  40.7 us
    all_to_all x2, blocking collectives, apply_operator(): lax.all_to_all(grouped, 'period', split_axis=0, concat_axis=0, tiled=True)  20.7 us
    all_to_all x2, blocking collectives, mix_periods(): lax.all_to_all(mixed_part, 'period', split_axis=0, concat_axis=0, tiled=T...  19.8 us
    all_to_all x1, blocking collectives, apply_operator(): lax.all_to_all(outgoing.astype(jnp.bfloat16), 'period', split_axis=0, con...  14 us
    all_to_all x1, blocking collectives, apply_operator(): lax.all_to_all(answers, 'period', split_axis=0, concat_axis=0, tiled=True)  10.4 us
  transfers between devices with their start and end apart: 7, of which 6 were waited for; matrix products, arithmetic and copies ran while one was open for 1% of the time, Pallas kernels for 0%

commit v1 on v0

v1 whole, which is shorter than its diff:
```python
import functools
import math

import jax
import jax.numpy as jnp
from jax import lax
from jax.experimental import pallas as pl
from jax.experimental.pallas import tpu as pltpu
from jax.sharding import PartitionSpec as P

epsilon = 1e-06
kernel_scale = 0.05
kernel_length = 6.0
highest = lax.Precision.HIGHEST
MESH = pl.DeviceIdType.MESH
F32 = jnp.float32
BF16 = jnp.bfloat16
LANES = 128
early_tiles = 4


def kernel(
    n,
    probes_ref,
    foot_hbm,
    lag_ref,
    owner_ref,
    tile_ref,
    coords_ref,
    temporal_ref,
    coef_ref,
    residual_ref,
    foot,
    pbuf,
    meta,
    terms,
    stats,
    flux_out,
    flux_in,
    image_out,
    image_in,
    kbuf,
    zt,
    foot_sem,
    pair_send,
    pair_recv,
    peer_send,
    peer_recv,
):
    me = lax.axis_index("period")
    half = lax.axis_index("half")
    blocks, probes_n, half_sounds = probes_ref.shape
    sounds, window = foot.shape[1:]
    win_tiles = window // LANES
    half_cells = coords_ref.shape[1] // 2
    tiles = half_cells // LANES
    rows = probes_n * blocks
    total = float(n * blocks * sounds)

    fetch = pltpu.make_async_copy(foot_hbm, foot, foot_sem)
    fetch.start()

    barrier = pltpu.get_barrier_semaphore()

    def greet(k, carry):
        pl.semaphore_signal(
            barrier, inc=1, device_id={"period": lax.rem(me + k, n)}, device_id_type=MESH
        )
        return carry

    lax.fori_loop(1, n, greet, 0)
    pl.semaphore_signal(barrier, inc=1, device_id={"half": 1 - half}, device_id_type=MESH)

    def pair_copy(source, target, which):
        return pltpu.make_async_remote_copy(
            src_ref=source,
            dst_ref=target,
            send_sem=pair_send.at[which],
            recv_sem=pair_recv.at[which],
            device_id={"half": 1 - half},
            device_id_type=MESH,
        )

    def peer_copy(slots, slot, which, k):
        return pltpu.make_async_remote_copy(
            src_ref=slots.at[slot],
            dst_ref=slots.at[slot],
            send_sem=peer_send.at[which, k],
            recv_sem=peer_recv.at[which, k],
            device_id={"period": lax.rem(me + k, n)},
            device_id_type=MESH,
        )

    def share(slots, which):
        def step(k, carry):
            peer_copy(slots, me, which, k).start()
            return carry

        lax.fori_loop(1, n, step, 0)

    def collect(slots, which):
        def step(k, carry):
            peer_copy(slots, lax.rem(me + n - k, n), which, k).wait_recv()
            return carry

        lax.fori_loop(1, n, step, 0)

    def drain(slots, which):
        def step(k, carry):
            peer_copy(slots, me, which, k).wait_send()
            return carry

        lax.fori_loop(1, n, step, 0)

    for p in range(probes_n):
        pbuf[half, p * blocks : (p + 1) * blocks, :] = probes_ref[:, p, :]

    span = meta.shape[2]
    lane = lax.broadcasted_iota(jnp.int32, (blocks, span), 1)
    weight = jnp.zeros((blocks, span), F32)
    for k in range(lag_ref.shape[1]):
        weight = weight + jnp.where(owner_ref[:, k : k + 1] == lane, lag_ref[:, k : k + 1], 0.0)
    tile_wide = jnp.broadcast_to(tile_ref[:, 0:1], (blocks, span))
    meta[me] = jnp.concatenate(
        [
            jnp.where(lane == span - 1, (tile_wide + j).astype(F32), weight)
            for j in range(win_tiles)
        ],
        axis=0,
    )

    pl.semaphore_wait(barrier, n)
    send_probes = pair_copy(pbuf.at[half], pbuf.at[half], 0)
    send_probes.start()
    share(meta, 0)

    length = math.log2(math.e) / kernel_length

    def cells(axis, start, count):
        picked = coords_ref[axis : axis + 1, pl.ds(pl.multiple_of(start, LANES), count)]
        return picked.astype(F32) * length

    out_x = cells(0, half * half_cells, half_cells)
    out_y = cells(1, half * half_cells, half_cells)
    wide = kbuf.shape[2]

    def build(i, carry):
        own = i < tiles
        side = jnp.where(own, half, 1 - half)
        start = side * half_cells + jnp.where(own, i, i - tiles) * LANES
        in_x = jnp.transpose(jnp.broadcast_to(cells(0, start, LANES), (LANES, LANES)))
        in_y = jnp.transpose(jnp.broadcast_to(cells(1, start, LANES), (LANES, LANES)))
        at = pl.multiple_of(i * LANES, LANES)
        for t in range(tiles):
            dx = in_x - out_x[:, t * LANES : (t + 1) * LANES]
            dy = in_y - out_y[:, t * LANES : (t + 1) * LANES]
            squared = dx * dx + dy * dy
            distance = squared * lax.rsqrt(jnp.maximum(squared, 1e-20))
            lo = t * LANES % wide
            kbuf[t * LANES // wide, pl.ds(at, LANES), lo : lo + LANES] = jnp.exp2(
                -distance
            ).astype(BF16)
        return carry

    lax.fori_loop(0, early_tiles, build, 0)

    row_block = lax.rem(lax.broadcasted_iota(jnp.int32, (rows, LANES), 0), blocks)

    def own_rows(values, b):
        keep = jnp.concatenate([row_block] * (values.shape[1] // LANES), axis=1) == b
        return jnp.where(keep, values, 0.0)

    def back(vector, step):
        part = jnp.zeros((rows, window), F32)
        for b in range(blocks):
            part = part + jnp.dot(
                own_rows(vector, b).astype(BF16), foot[b], preferred_element_type=F32
            )
        by_tile = [
            jnp.concatenate(
                [
                    part[p * blocks : (p + 1) * blocks, j * LANES : (j + 1) * LANES]
                    for p in range(probes_n)
                ],
                axis=1,
            )
            for j in range(win_tiles)
        ]
        terms[step, me] = jnp.concatenate(by_tile, axis=0).astype(BF16)
        share(terms.at[step], 1 + step)

    tile_rows = jnp.concatenate(
        [jnp.broadcast_to(tile_ref[:, 0:1], (blocks, LANES))] * probes_n, axis=0
    )

    def forth(mixer, step):
        collect(terms.at[step], 1 + step)
        shared = terms[step].reshape(n * win_tiles * blocks, probes_n * LANES)
        flux = jnp.dot(mixer[0], shared, preferred_element_type=F32) + jnp.dot(
            mixer[1], shared, preferred_element_type=F32
        )
        flux_out[step] = jnp.concatenate(
            [
                jnp.concatenate(
                    [
                        flux[t * blocks : (t + 1) * blocks, p * LANES : (p + 1) * LANES]
                        for t in range(tiles)
                    ],
                    axis=1,
                )
                for p in range(probes_n)
            ],
            axis=0,
        ).astype(BF16)
        swap = pair_copy(flux_out.at[step], flux_in.at[step], 1 + 2 * step)
        swap.start()
        each = wide // LANES

        def own_part(c, carry):
            got = jnp.dot(
                flux_out[step], kbuf[c, 0:half_cells, :], preferred_element_type=F32
            )
            for e in range(each):
                zt[c * each + e] = got[:, e * LANES : (e + 1) * LANES]
            return carry

        def other_part(c, carry):
            got = jnp.dot(
                flux_in[step],
                kbuf[c, half_cells : 2 * half_cells, :],
                preferred_element_type=F32,
            )
            for e in range(each):
                zt[c * each + e] += got[:, e * LANES : (e + 1) * LANES]
            return carry

        lax.fori_loop(0, kbuf.shape[0], own_part, 0)
        swap.wait()
        lax.fori_loop(0, kbuf.shape[0], other_part, 0)
        parts = []
        for j in range(win_tiles):
            picked = jnp.zeros((rows, LANES), F32)
            for t in range(tiles):
                picked = jnp.where(tile_rows + j == t, zt[t], picked)
            parts.append(picked)
        windows = jnp.concatenate(parts, axis=1)
        image = jnp.zeros((rows, sounds), F32)
        for b in range(blocks):
            image = image + lax.dot_general(
                own_rows(windows, b).astype(BF16),
                foot[b],
                (((1,), (1,)), ((), ())),
                preferred_element_type=F32,
            )
        image_out[step] = image
        swap = pair_copy(image_out.at[step], image_in.at[step], 2 + 2 * step)
        swap.start()
        swap.wait()
        return image + image_in[step]

    def folded(left, right):
        products = left * right
        wide_sum = products[:, 0:LANES]
        for e in range(1, sounds // LANES):
            wide_sum = wide_sum + products[:, e * LANES : (e + 1) * LANES]
        return [
            jnp.sum(wide_sum[p * blocks : (p + 1) * blocks], axis=0, keepdims=True)
            for p in range(probes_n)
        ]

    def start_sums(pairs, step):
        found = []
        for left, right in pairs:
            found += folded(left, right)
        found.append(jnp.zeros((stats.shape[2] - len(found), LANES), F32))
        stats[step, me] = jnp.concatenate(found, axis=0)
        share(stats.at[step], 3 + step)

    def end_sums(step):
        collect(stats.at[step], 3 + step)
        summed = jnp.sum(jnp.sum(stats[step], axis=0), axis=1, keepdims=True)
        return [summed[k * probes_n : (k + 1) * probes_n] for k in range(3)]

    def spread(values):
        return jnp.concatenate(
            [jnp.broadcast_to(values[p : p + 1, :], (blocks, sounds)) for p in range(probes_n)],
            axis=0,
        )

    fetch.wait()
    send_probes.wait_recv()
    probe = jnp.concatenate([pbuf[0], pbuf[1]], axis=1)
    back(probe, 0)

    lax.fori_loop(early_tiles, 2 * tiles, build, 0)

    collect(meta, 0)
    weight_rows = meta[me, 0:blocks, 0:n]
    mixed = jnp.dot(weight_rows, temporal_ref[...], precision=highest, preferred_element_type=F32)
    if span > n:
        mixed = jnp.concatenate([mixed, jnp.zeros((blocks, span - n), F32)], axis=1)
    asks = jnp.concatenate([mixed, jnp.where(lane == span - 1, 1.0, 0.0)], axis=0)
    every = meta[...].reshape(n * win_tiles * blocks, span)
    answer = lax.dot_general(
        asks, every, (((1,), (1,)), ((), ())), precision=highest, preferred_element_type=F32
    )
    gram = answer[0:blocks] * kernel_scale
    place = answer[blocks : 2 * blocks]
    mixer = jnp.concatenate(
        [jnp.where(jnp.abs(place - t) < 0.5, gram, 0.0) for t in range(tiles)], axis=0
    )
    mixer_high = mixer.astype(BF16)
    mixer_pair = (mixer_high, (mixer - mixer_high.astype(F32)).astype(BF16))

    image = forth(mixer_pair, 0)
    back(image, 1)
    start_sums([(probe, probe), (probe, image), (image, image)], 0)
    second = forth(mixer_pair, 1)
    pp, pw, ww = end_sums(0)
    scale = jnp.sqrt(pp / total + epsilon)
    alpha_one = pw / (scale * scale * total)
    rest = (ww - 2.0 * alpha_one * pw + alpha_one * alpha_one * pp) / (scale * scale * total)
    beta_one = jnp.sqrt(jnp.maximum(rest, 0.0) + epsilon)
    shrink = spread(1.0 / (scale * beta_one))
    alpha_wide = spread(alpha_one)
    next_q = (image - alpha_wide * probe) * shrink
    next_w = (second - alpha_wide * image) * shrink - spread(beta_one / scale) * probe
    start_sums([(next_q, next_w), (next_w, next_w), (next_q, next_q)], 1)
    qw, ww, qq = end_sums(1)
    alpha_two = qw / total
    rest = (ww - 2.0 * alpha_two * qw + alpha_two * alpha_two * qq) / total
    beta_two = jnp.sqrt(jnp.maximum(rest, 0.0) + epsilon)
    residual = next_w - spread(alpha_two) * next_q
    own = jnp.where(half == 0, residual[:, 0:half_sounds], residual[:, half_sounds:])
    for p in range(probes_n):
        residual_ref[:, p, :] = own[p * blocks : (p + 1) * blocks]
    shape = (probes_n, probes_n)
    corner = lax.broadcasted_iota(jnp.int32, shape, 0) == lax.broadcasted_iota(jnp.int32, shape, 1)
    for k, column in enumerate([alpha_one, beta_one, alpha_two, beta_two]):
        coef_ref[k : k + 1, :] = jnp.sum(
            jnp.where(corner, jnp.broadcast_to(column, shape), 0.0), axis=0, keepdims=True
        )

    send_probes.wait_send()
    drain(meta, 0)
    for step in range(2):
        drain(terms.at[step], 1 + step)
        drain(stats.at[step], 3 + step)


def body(probes, footprints, lag_weights, owners, window_tiles, coords, temporal):
    n = lax.axis_size("period")
    blocks, probes_n, half_sounds = probes.shape
    sounds, window = footprints.shape[1:]
    half_cells = coords.shape[1] // 2
    tiles = half_cells // LANES
    rows = probes_n * blocks
    span = LANES * -(-(n + 1) // LANES)
    entries = window // LANES * blocks
    wide = 2 * LANES if tiles % 2 == 0 else LANES
    stat_rows = 8 * -(-3 * probes_n // 8)
    vmem = pl.BlockSpec(memory_space=pltpu.VMEM)
    return pl.pallas_call(
        functools.partial(kernel, n),
        out_shape=(
            jax.ShapeDtypeStruct((4, probes_n), F32),
            jax.ShapeDtypeStruct(probes.shape, F32),
        ),
        in_specs=[vmem, pl.BlockSpec(memory_space=pl.ANY)] + [vmem] * 5,
        out_specs=(vmem, vmem),
        scratch_shapes=[
            pltpu.VMEM(footprints.shape, BF16),
            pltpu.VMEM((2, rows, half_sounds), F32),
            pltpu.VMEM((n, entries, span), F32),
            pltpu.VMEM((2, n, entries, probes_n * LANES), BF16),
            pltpu.VMEM((2, n, stat_rows, LANES), F32),
            pltpu.VMEM((2, rows, half_cells), BF16),
            pltpu.VMEM((2, rows, half_cells), BF16),
            pltpu.VMEM((2, rows, sounds), F32),
            pltpu.VMEM((2, rows, sounds), F32),
            pltpu.VMEM((half_cells // wide, 2 * half_cells, wide), BF16),
            pltpu.VMEM((tiles, rows, LANES), F32),
            pltpu.SemaphoreType.DMA,
            pltpu.SemaphoreType.DMA((5,)),
            pltpu.SemaphoreType.DMA((5,)),
            pltpu.SemaphoreType.DMA((5, n)),
            pltpu.SemaphoreType.DMA((5, n)),
        ],
        compiler_params=pltpu.CompilerParams(
            collective_id=0, has_side_effects=True, vmem_limit_bytes=48 * 1024 * 1024
        ),
    )(probes, footprints, lag_weights, owners, window_tiles, coords, temporal)


def solution(mesh):
    in_specs = (
        P("period", None, "half"),
        P("period", None, "half"),
        P("period", None),
        P("period", None),
        P("period", "half"),
        P(),
        P(),
    )
    out_specs = (P(), P("period", None, "half"))
    return jax.shard_map(body, mesh=mesh, in_specs=in_specs, out_specs=out_specs, check_vma=False)
```

time: 440 us -> 53.6 us (0.12)
  blocking collectives: 270 us -> 0 us
  matrix products: 91.7 us -> 0 us
  Pallas kernels: 0 us -> 45.3 us
  waiting for transfers between devices: 27 us -> 0 us
  starting transfers between devices: 17.5 us -> 0 us
  between operations: 14.4 us -> 0.64 us
  local copies, waits for them, and re-layouts: 13.6 us -> 7.22 us
    psum x5 -> x0, blocking collectives: 202 us -> none  [the longest x2 81.1 us: lanczos_step(): inner_sum = lax.psum(local_mean(current * image), ('period', 'half'))]
    dot_general x18 -> x0, matrix products: 91.7 us -> none  [the longest x2 85.9 us: apply_operator(): jnp.einsum('pc,gkc->gpk', whole_flux, kernel_rows, precision=highest)]
    all_to_all x6 -> x0, blocking collectives: 64.8 us -> none  [the longest x2 20.7 us: apply_operator(): lax.all_to_all(grouped, 'period', split_axis=0, concat_axis=0, tiled=True)]
    pallas_call x0 -> x1, Pallas kernels: none -> 45.3 us  [body(): pl.pallas_call(functools.partial(kernel, n), out_shape=(jax.ShapeDtypeStr...]
    all_to_all x3 -> x0, starting transfers between devices: 17.2 us -> none  [the longest x1 8.31 us: body(): lax.all_to_all(wanted, 'period', split_axis=0, concat_axis=0, tiled=True)]
    all_to_all x3 -> x0, waiting for transfers between devices: 15.3 us -> none  [the longest x1 7.71 us: apply_operator(): lax.all_to_all(outgoing.astype(jnp.bfloat16), 'period', split_axis=0, con...]
    unnamed x4 -> x0, waiting for transfers between devices: 9.59 us -> none
    unnamed x23 -> x13, local copies, waits for them, and re-layouts: 9.05 us -> 7.22 us
  transfers between devices with their start and end apart: 7 -> 0, of which waited for: 6 -> 0; matrix products, arithmetic and copies ran while one was open for 1% -> 0% of each run, Pallas kernels for 0% -> 0%
where the time goes in v1:
time: 53.6 us; the launch traced here: 53.2 us
  Pallas kernels  45.3 us (85%)
  local copies, waits for them, and re-layouts  7.22 us (13%)
  between operations  0.64 us (1%)
    pallas_call x1, Pallas kernels, body(): pl.pallas_call(functools.partial(kernel, n), out_shape=(jax.ShapeDtypeStr...  45.3 us
    unnamed x13, local copies, waits for them, and re-layouts  7.22 us

profile of v1, /device:TPU:0, one launch (start us, length us, event | category | flops | bytes accessed | tf_op | source)
XLA Modules:
  0.0 53.2 jit_solution(13174492190910251863)
XLA Ops:
  0.6 0.8 %copy.9.lag_ref = f32[8,4]{1,0:T(8,128)S(1)} copy(f32[8,4]{0,1:T(4,128)} %param.9) | data formatting | bytes 256 | tf_op args[2]
  1.4 0.8 %copy.10.owner_ref = s32[8,4]{1,0:T(8,128)S(1)} copy(s32[8,4]{0,1:T(4,128)} %param.10) | data formatting | bytes 256 | tf_op args[3]
  2.1 0.7 %copy.11.tile_ref = s32[8,1]{1,0:T(8,128)S(1)} copy(s32[8,1]{0,1:T(1,128)} %param.11) | data formatting | bytes 64 | tf_op args[4]
  2.9 0.0 copy-start
  2.9 1.6 %copy-done = bf16[8,512,256]{2,1,0:T(8,128)(2,1)S(1)} copy-done((bf16[8,512,256]{2,1,0:T(8,128)(2,1)S(1)}, bf16[8,512,256]{2,1,0:T(8,128)(2,1)}, u32[]{:S(2)}) %copy-start) | copy-done | bytes 2097176
  4.5 0.0 copy-start.1
  4.5 0.8 %copy-done.1 = f32[8,4,256]{2,1,0:T(4,128)S(1)} copy-done((f32[8,4,256]{2,1,0:T(4,128)S(1)}, f32[8,4,256]{2,1,0:T(4,128)}, u32[]{:S(2)}) %copy-start.1) | copy-done | bytes 32792
  5.2 0.0 copy-start.2
  5.2 0.7 %copy-done.2 = s32[2,3072]{1,0:T(2,128)S(1)} copy-done((s32[2,3072]{1,0:T(2,128)S(1)}, s32[2,3072]{1,0:T(2,128)}, u32[]{:S(2)}) %copy-start.2) | copy-done | bytes 24600
  6.0 0.0 copy-start.3
  6.0 0.7 %copy-done.3 = f32[16,16]{1,0:T(8,128)S(1)} copy-done((f32[16,16]{1,0:T(8,128)S(1)}, f32[16,16]{1,0:T(8,128)}, u32[]{:S(2)}) %copy-start.3) | copy-done | bytes 1048
  6.7 45.3 %shard_map.86 = (f32[4,4]{1,0:T(4,128)S(1)}, f32[8,4,256]{2,1,0:T(4,128)S(1)}) custom-call(f32[8,4,256]{2,1,0:T(4,128)S(1)} %copy-done.1, bf16[8,512,256]{2,1,0:T(8,128)(2,1)S(1)} %copy-done, f32[8,4]{1,0:T(8,128)S(1)} %copy.9.lag_ref, s32[8,4]{1,0:T(8,128)S(1)} %copy.10.owner_ref, s32[8,1]{1,0:T(8,128)S(1)} %copy.11.tile_ref, s32[2,3072]{1,0:T(2,128)S(1)} %copy-done.2, ...), custom_call_target="tpu_custom_call" | custom-call | tf_op jit(solution)/shard_map/pallas_call | solution.py:363
  52.0 0.6 %copy.14 = f32[4,4]{1,0:T(4,128)} copy(f32[4,4]{1,0:T(4,128)S(1)} %get-tuple-element.4) | data formatting | bytes 128
  52.6 0.6 %copy.15 = f32[8,4,256]{2,1,0:T(4,128)} copy(f32[8,4,256]{2,1,0:T(4,128)S(1)} %get-tuple-element.5) | data formatting | bytes 65536
Async XLA Ops:
  2.9 1.6 %copy-start = (bf16[8,512,256]{2,1,0:T(8,128)(2,1)S(1)}, bf16[8,512,256]{2,1,0:T(8,128)(2,1)}, u32[]{:S(2)}) copy-start(bf16[8,512,256]{2,1,0:T(8,128)(2,1)} %foot_hbm.1) | copy-start | bytes 6291460
  4.5 0.8 %copy-start.1 = (f32[8,4,256]{2,1,0:T(4,128)S(1)}, f32[8,4,256]{2,1,0:T(4,128)}, u32[]{:S(2)}) copy-start(f32[8,4,256]{2,1,0:T(4,128)} %probes_ref.1) | copy-start | bytes 98308
  5.2 0.7 %copy-start.2 = (s32[2,3072]{1,0:T(2,128)S(1)}, s32[2,3072]{1,0:T(2,128)}, u32[]{:S(2)}) copy-start(s32[2,3072]{1,0:T(2,128)} %coords_ref.1) | copy-start | bytes 73732
  6.0 0.7 %copy-start.3 = (f32[16,16]{1,0:T(8,128)S(1)}, f32[16,16]{1,0:T(8,128)}, u32[]{:S(2)}) copy-start(f32[16,16]{1,0:T(8,128)} %temporal_ref.1) | copy-start | bytes 3076

commit v2 on v1

--- a/solution.py
+++ b/solution.py
@@ -16,21 +16,28 @@
 F32 = jnp.float32
 BF16 = jnp.bfloat16
 LANES = 128
-early_tiles = 4
+first_tiles = 5
+early_tiles = 9
 
 
 def kernel(
     n,
+    probes_hbm,
+    foot_hbm,
+    lag_hbm,
+    owner_hbm,
+    tile_hbm,
+    coords_hbm,
+    temporal_hbm,
+    coef_ref,
+    residual_ref,
     probes_ref,
-    foot_hbm,
+    foot,
     lag_ref,
     owner_ref,
     tile_ref,
     coords_ref,
     temporal_ref,
-    coef_ref,
-    residual_ref,
-    foot,
     pbuf,
     meta,
     terms,
@@ -41,7 +48,8 @@
     image_in,
     kbuf,
     zt,
-    foot_sem,
+    features,
+    fetch_sem,
     pair_send,
     pair_recv,
     peer_send,
@@ -57,8 +65,21 @@
     rows = probes_n * blocks
     total = float(n * blocks * sounds)
 
-    fetch = pltpu.make_async_copy(foot_hbm, foot, foot_sem)
-    fetch.start()
+    arguments = [
+        (coords_hbm, coords_ref),
+        (probes_hbm, probes_ref),
+        (lag_hbm, lag_ref),
+        (owner_hbm, owner_ref),
+        (tile_hbm, tile_ref),
+        (temporal_hbm, temporal_ref),
+        (foot_hbm, foot),
+    ]
+    fetches = [
+        pltpu.make_async_copy(source, target, fetch_sem.at[k])
+        for k, (source, target) in enumerate(arguments)
+    ]
+    for fetch in fetches:
+        fetch.start()
 
     barrier = pltpu.get_barrier_semaphore()
 
@@ -112,57 +133,69 @@
 
         lax.fori_loop(1, n, step, 0)
 
+    fetches[0].wait()
+    x, y = coords_ref[0:1, :], coords_ref[1:2, :]
+    square = x * x + y * y
+    upper = jnp.bitwise_and(square, -64)
+    ones = jnp.ones_like(x)
+    blank = jnp.zeros((LANES - 6, x.shape[1]), F32)
+
+    def feature_rows(parts):
+        return jnp.concatenate([part.astype(F32) for part in parts] + [blank], axis=0)
+
+    features[0] = feature_rows([x * -2, y * -2, upper, square - upper, ones, ones])
+    features[1] = feature_rows([x, y, ones, ones, upper, square - upper])
+    wide = kbuf.shape[2]
+    own_start = pl.multiple_of(half * half_cells, LANES)
+    rate = -math.log2(math.e) / kernel_length
+
+    def build(i, carry):
+        own = i < tiles
+        side = jnp.where(own, half, 1 - half)
+        start = side * half_cells + jnp.where(own, i, i - tiles) * LANES
+        left = jnp.transpose(features[0, :, pl.ds(pl.multiple_of(start, LANES), LANES)])
+        left = left.astype(BF16)
+        at = pl.multiple_of(i * LANES, LANES)
+        for c in range(kbuf.shape[0]):
+            right = features[
+                1, :, pl.ds(pl.multiple_of(own_start + c * wide, LANES), wide)
+            ].astype(BF16)
+            squared = jnp.dot(left, right, preferred_element_type=F32)
+            power = squared * rate * lax.rsqrt(jnp.maximum(squared, 0.5))
+            kbuf[c, pl.ds(at, LANES), :] = jnp.exp2(power).astype(BF16)
+        return carry
+
+    lax.fori_loop(0, first_tiles, build, 0)
+
+    for fetch in fetches[1:6]:
+        fetch.wait()
     for p in range(probes_n):
         pbuf[half, p * blocks : (p + 1) * blocks, :] = probes_ref[:, p, :]
 
     span = meta.shape[2]
     lane = lax.broadcasted_iota(jnp.int32, (blocks, span), 1)
+    square_shape = (blocks, blocks)
+    diagonal = lax.broadcasted_iota(jnp.int32, square_shape, 0) == lax.broadcasted_iota(
+        jnp.int32, square_shape, 1
+    )
+
+    def upright(row):
+        spread_row = jnp.broadcast_to(row.astype(F32), square_shape)
+        return jnp.sum(jnp.where(diagonal, spread_row, 0.0), axis=1, keepdims=True)
+
     weight = jnp.zeros((blocks, span), F32)
-    for k in range(lag_ref.shape[1]):
-        weight = weight + jnp.where(owner_ref[:, k : k + 1] == lane, lag_ref[:, k : k + 1], 0.0)
-    tile_wide = jnp.broadcast_to(tile_ref[:, 0:1], (blocks, span))
-    meta[me] = jnp.concatenate(
-        [
-            jnp.where(lane == span - 1, (tile_wide + j).astype(F32), weight)
-            for j in range(win_tiles)
-        ],
-        axis=0,
-    )
+    for k in range(lag_ref.shape[0]):
+        chosen = upright(owner_ref[k : k + 1, :]) == lane.astype(F32)
+        weight = weight + jnp.where(chosen, upright(lag_ref[k : k + 1, :]), 0.0)
+    tile_column = upright(tile_ref[0:1, :])
+    meta[me] = jnp.where(lane == span - 1, tile_column, weight)
 
     pl.semaphore_wait(barrier, n)
     send_probes = pair_copy(pbuf.at[half], pbuf.at[half], 0)
     send_probes.start()
     share(meta, 0)
 
-    length = math.log2(math.e) / kernel_length
-
-    def cells(axis, start, count):
-        picked = coords_ref[axis : axis + 1, pl.ds(pl.multiple_of(start, LANES), count)]
-        return picked.astype(F32) * length
-
-    out_x = cells(0, half * half_cells, half_cells)
-    out_y = cells(1, half * half_cells, half_cells)
-    wide = kbuf.shape[2]
-
-    def build(i, carry):
-        own = i < tiles
-        side = jnp.where(own, half, 1 - half)
-        start = side * half_cells + jnp.where(own, i, i - tiles) * LANES
-        in_x = jnp.transpose(jnp.broadcast_to(cells(0, start, LANES), (LANES, LANES)))
-        in_y = jnp.transpose(jnp.broadcast_to(cells(1, start, LANES), (LANES, LANES)))
-        at = pl.multiple_of(i * LANES, LANES)
-        for t in range(tiles):
-            dx = in_x - out_x[:, t * LANES : (t + 1) * LANES]
-            dy = in_y - out_y[:, t * LANES : (t + 1) * LANES]
-            squared = dx * dx + dy * dy
-            distance = squared * lax.rsqrt(jnp.maximum(squared, 1e-20))
-            lo = t * LANES % wide
-            kbuf[t * LANES // wide, pl.ds(at, LANES), lo : lo + LANES] = jnp.exp2(
-                -distance
-            ).astype(BF16)
-        return carry
-
-    lax.fori_loop(0, early_tiles, build, 0)
+    lax.fori_loop(first_tiles, early_tiles, build, 0)
 
     row_block = lax.rem(lax.broadcasted_iota(jnp.int32, (rows, LANES), 0), blocks)
 
@@ -190,7 +223,7 @@
         share(terms.at[step], 1 + step)
 
     tile_rows = jnp.concatenate(
-        [jnp.broadcast_to(tile_ref[:, 0:1], (blocks, LANES))] * probes_n, axis=0
+        [jnp.broadcast_to(tile_column, (blocks, LANES))] * probes_n, axis=0
     )
 
     def forth(mixer, step):
@@ -241,7 +274,7 @@
         for j in range(win_tiles):
             picked = jnp.zeros((rows, LANES), F32)
             for t in range(tiles):
-                picked = jnp.where(tile_rows + j == t, zt[t], picked)
+                picked = jnp.where(jnp.abs(tile_rows + float(j - t)) < 0.5, zt[t], picked)
             parts.append(picked)
         windows = jnp.concatenate(parts, axis=1)
         image = jnp.zeros((rows, sounds), F32)
@@ -272,14 +305,22 @@
         found = []
         for left, right in pairs:
             found += folded(left, right)
-        found.append(jnp.zeros((stats.shape[2] - len(found), LANES), F32))
-        stats[step, me] = jnp.concatenate(found, axis=0)
+        shape = (len(found), LANES)
+        place = lax.broadcasted_iota(jnp.int32, shape, 1) == lax.broadcasted_iota(
+            jnp.int32, shape, 0
+        )
+        sums = jnp.sum(jnp.concatenate(found, axis=0), axis=1, keepdims=True)
+        stats[step, me] = jnp.sum(jnp.where(place, sums, 0.0), axis=0, keepdims=True)
         share(stats.at[step], 3 + step)
 
     def end_sums(step):
         collect(stats.at[step], 3 + step)
-        summed = jnp.sum(jnp.sum(stats[step], axis=0), axis=1, keepdims=True)
-        return [summed[k * probes_n : (k + 1) * probes_n] for k in range(3)]
+        summed = jnp.broadcast_to(jnp.sum(stats[step], axis=0), (3 * probes_n, LANES))
+        place = lax.broadcasted_iota(jnp.int32, summed.shape, 1) == lax.broadcasted_iota(
+            jnp.int32, summed.shape, 0
+        )
+        found = jnp.sum(jnp.where(place, summed, 0.0), axis=1, keepdims=True)
+        return [found[k * probes_n : (k + 1) * probes_n] for k in range(3)]
 
     def spread(values):
         return jnp.concatenate(
@@ -287,7 +328,7 @@
             axis=0,
         )
 
-    fetch.wait()
+    fetches[6].wait()
     send_probes.wait_recv()
     probe = jnp.concatenate([pbuf[0], pbuf[1]], axis=1)
     back(probe, 0)
@@ -300,7 +341,10 @@
     if span > n:
         mixed = jnp.concatenate([mixed, jnp.zeros((blocks, span - n), F32)], axis=1)
     asks = jnp.concatenate([mixed, jnp.where(lane == span - 1, 1.0, 0.0)], axis=0)
-    every = meta[...].reshape(n * win_tiles * blocks, span)
+    last = lax.broadcasted_iota(jnp.int32, (n, blocks, span), 2) == span - 1
+    every = jnp.stack(
+        [meta[...] + jnp.where(last, float(j), 0.0) for j in range(win_tiles)], axis=1
+    ).reshape(n * win_tiles * blocks, span)
     answer = lax.dot_general(
         asks, every, (((1,), (1,)), ((), ())), precision=highest, preferred_element_type=F32
     )
@@ -358,7 +402,15 @@
     span = LANES * -(-(n + 1) // LANES)
     entries = window // LANES * blocks
     wide = 2 * LANES if tiles % 2 == 0 else LANES
-    stat_rows = 8 * -(-3 * probes_n // 8)
+    arguments = (
+        probes,
+        footprints,
+        lag_weights.T,
+        owners.T,
+        window_tiles.T,
+        coords,
+        temporal,
+    )
     vmem = pl.BlockSpec(memory_space=pltpu.VMEM)
     return pl.pallas_call(
         functools.partial(kernel, n),
@@ -366,21 +418,22 @@
             jax.ShapeDtypeStruct((4, probes_n), F32),
             jax.ShapeDtypeStruct(probes.shape, F32),
         ),
-        in_specs=[vmem, pl.BlockSpec(memory_space=pl.ANY)] + [vmem] * 5,
+        in_specs=[pl.BlockSpec(memory_space=pltpu.HBM)] * len(arguments),
         out_specs=(vmem, vmem),
         scratch_shapes=[
-            pltpu.VMEM(footprints.shape, BF16),
+            *[pltpu.VMEM(argument.shape, argument.dtype) for argument in arguments],
             pltpu.VMEM((2, rows, half_sounds), F32),
-            pltpu.VMEM((n, entries, span), F32),
+            pltpu.VMEM((n, blocks, span), F32),
             pltpu.VMEM((2, n, entries, probes_n * LANES), BF16),
-            pltpu.VMEM((2, n, stat_rows, LANES), F32),
+            pltpu.VMEM((2, n, 1, LANES), F32),
             pltpu.VMEM((2, rows, half_cells), BF16),
             pltpu.VMEM((2, rows, half_cells), BF16),
             pltpu.VMEM((2, rows, sounds), F32),
             pltpu.VMEM((2, rows, sounds), F32),
             pltpu.VMEM((half_cells // wide, 2 * half_cells, wide), BF16),
             pltpu.VMEM((tiles, rows, LANES), F32),
-            pltpu.SemaphoreType.DMA,
+            pltpu.VMEM((2, LANES, 2 * half_cells), F32),
+            pltpu.SemaphoreType.DMA((len(arguments),)),
             pltpu.SemaphoreType.DMA((5,)),
             pltpu.SemaphoreType.DMA((5,)),
             pltpu.SemaphoreType.DMA((5, n)),
@@ -389,7 +442,7 @@
         compiler_params=pltpu.CompilerParams(
             collective_id=0, has_side_effects=True, vmem_limit_bytes=48 * 1024 * 1024
         ),
-    )(probes, footprints, lag_weights, owners, window_tiles, coords, temporal)
+    )(*arguments)
 
 
 def solution(mesh):

time: 53.6 us -> 51.4 us (0.959)
  Pallas kernels: 45.3 us -> 43.3 us
    pallas_call x1, Pallas kernels: 45.3 us -> 43.3 us  [body(): pl.pallas_call(functools.partial(kernel, n), out_shape=(jax.ShapeDtypeStr...]
    unnamed x13 -> x16, local copies, waits for them, and re-layouts: 7.22 us -> 6.99 us
where the time goes in v2:
time: 51.4 us; the launch traced here: 51 us
  Pallas kernels  43.3 us (84%)
  local copies, waits for them, and re-layouts  6.99 us (14%)
  between operations  0.66 us (1%)
    pallas_call x1, Pallas kernels, body(): pl.pallas_call(functools.partial(kernel, n), out_shape=(jax.ShapeDtypeStr...  43.3 us
    unnamed x16, local copies, waits for them, and re-layouts  6.99 us

profile of v2, /device:TPU:0, one launch (start us, length us, event | category | flops | bytes accessed | tf_op | source)
XLA Modules:
  0.0 51.0 jit_solution(8502114826656332440)
XLA Ops:
  0.6 0.0 copy-start
  0.6 1.6 %copy-done = bf16[8,512,256]{2,1,0:T(8,128)(2,1)S(1)} copy-done((bf16[8,512,256]{2,1,0:T(8,128)(2,1)S(1)}, bf16[8,512,256]{2,1,0:T(8,128)(2,1)}, u32[]{:S(2)}) %copy-start) | copy-done | bytes 2097176
  2.2 0.0 copy-start.1
  2.2 0.8 %copy-done.1 = f32[8,4,256]{2,1,0:T(4,128)S(1)} copy-done((f32[8,4,256]{2,1,0:T(4,128)S(1)}, f32[8,4,256]{2,1,0:T(4,128)}, u32[]{:S(2)}) %copy-start.1) | copy-done | bytes 32792
  3.0 0.0 copy-start.2
  3.0 0.7 %copy-done.2 = s32[2,3072]{1,0:T(2,128)S(1)} copy-done((s32[2,3072]{1,0:T(2,128)S(1)}, s32[2,3072]{1,0:T(2,128)}, u32[]{:S(2)}) %copy-start.2) | copy-done | bytes 24600
  3.7 0.0 copy-start.3
  3.7 0.7 %copy-done.3 = f32[16,16]{1,0:T(8,128)S(1)} copy-done((f32[16,16]{1,0:T(8,128)S(1)}, f32[16,16]{1,0:T(8,128)}, u32[]{:S(2)}) %copy-start.3) | copy-done | bytes 1048
  4.4 0.0 copy-start.4
  4.4 0.7 %copy-done.4 = f32[8,4]{0,1:T(4,128)S(1)} copy-done((f32[8,4]{0,1:T(4,128)S(1)}, f32[8,4]{0,1:T(4,128)}, u32[]{:S(2)}) %copy-start.4) | copy-done | bytes 152
  5.1 0.0 copy-start.5
  5.1 0.7 %copy-done.5 = s32[8,4]{0,1:T(4,128)S(1)} copy-done((s32[8,4]{0,1:T(4,128)S(1)}, s32[8,4]{0,1:T(4,128)}, u32[]{:S(2)}) %copy-start.5) | copy-done | bytes 152
  5.8 0.0 copy-start.6
  5.8 0.7 %copy-done.6 = s32[8,1]{0,1:T(1,128)S(1)} copy-done((s32[8,1]{0,1:T(1,128)S(1)}, s32[8,1]{0,1:T(1,128)}, u32[]{:S(2)}) %copy-start.6) | copy-done | bytes 56
  6.4 43.3 %shard_map.86 = (f32[4,4]{1,0:T(4,128)S(1)}, f32[8,4,256]{2,1,0:T(4,128)S(1)}) custom-call(f32[8,4,256]{2,1,0:T(4,128)S(1)} %copy-done.1, bf16[8,512,256]{2,1,0:T(8,128)(2,1)S(1)} %copy-done, f32[4,8]{1,0:T(4,128)S(1)} %bitcast.3, s32[4,8]{1,0:T(4,128)S(1)} %bitcast.4, s32[1,8]{1,0:T(1,128)S(1)} %bitcast.5, s32[2,3072]{1,0:T(2,128)S(1)} %copy-done.2, ...), custom_call_target="tpu_custom_call" | custom-call | tf_op jit(solution)/shard_map/pallas_call | solution.py:415
  49.8 0.6 %copy.11 = f32[4,4]{1,0:T(4,128)} copy(f32[4,4]{1,0:T(4,128)S(1)} %get-tuple-element.4) | data formatting | bytes 128
  50.4 0.6 %copy.12 = f32[8,4,256]{2,1,0:T(4,128)} copy(f32[8,4,256]{2,1,0:T(4,128)S(1)} %get-tuple-element.5) | data formatting | bytes 65536
Async XLA Ops:
  0.6 1.6 %copy-start = (bf16[8,512,256]{2,1,0:T(8,128)(2,1)S(1)}, bf16[8,512,256]{2,1,0:T(8,128)(2,1)}, u32[]{:S(2)}) copy-start(bf16[8,512,256]{2,1,0:T(8,128)(2,1)} %foot_hbm.1) | copy-start | bytes 6291460
  2.2 0.8 %copy-start.1 = (f32[8,4,256]{2,1,0:T(4,128)S(1)}, f32[8,4,256]{2,1,0:T(4,128)}, u32[]{:S(2)}) copy-start(f32[8,4,256]{2,1,0:T(4,128)} %probes_hbm.1) | copy-start | bytes 98308
  3.0 0.7 %copy-start.2 = (s32[2,3072]{1,0:T(2,128)S(1)}, s32[2,3072]{1,0:T(2,128)}, u32[]{:S(2)}) copy-start(s32[2,3072]{1,0:T(2,128)} %coords_hbm.1) | copy-start | bytes 73732
  3.7 0.7 %copy-start.3 = (f32[16,16]{1,0:T(8,128)S(1)}, f32[16,16]{1,0:T(8,128)}, u32[]{:S(2)}) copy-start(f32[16,16]{1,0:T(8,128)} %temporal_hbm.1) | copy-start | bytes 3076
  4.4 0.7 %copy-start.4 = (f32[8,4]{0,1:T(4,128)S(1)}, f32[8,4]{0,1:T(4,128)}, u32[]{:S(2)}) copy-start(f32[8,4]{0,1:T(4,128)} %param.9) | copy-start | bytes 388
  5.1 0.7 %copy-start.5 = (s32[8,4]{0,1:T(4,128)S(1)}, s32[8,4]{0,1:T(4,128)}, u32[]{:S(2)}) copy-start(s32[8,4]{0,1:T(4,128)} %param.10) | copy-start | bytes 388
  5.8 0.7 %copy-start.6 = (s32[8,1]{0,1:T(1,128)S(1)}, s32[8,1]{0,1:T(1,128)}, u32[]{:S(2)}) copy-start(s32[8,1]{0,1:T(1,128)} %param.11) | copy-start | bytes 100

commit v3 on v2

--- a/solution.py
+++ b/solution.py
@@ -47,7 +47,6 @@
     image_out,
     image_in,
     kbuf,
-    zt,
     features,
     fetch_sem,
     pair_send,
@@ -249,27 +248,25 @@
         swap.start()
         each = wide // LANES
 
-        def own_part(c, carry):
-            got = jnp.dot(
-                flux_out[step], kbuf[c, 0:half_cells, :], preferred_element_type=F32
-            )
-            for e in range(each):
-                zt[c * each + e] = got[:, e * LANES : (e + 1) * LANES]
-            return carry
-
-        def other_part(c, carry):
-            got = jnp.dot(
+        columns = kbuf.shape[0]
+        spatial = [
+            jnp.dot(flux_out[step], kbuf[c, 0:half_cells, :], preferred_element_type=F32)
+            for c in range(columns)
+        ]
+        swap.wait()
+        spatial = [
+            spatial[c]
+            + jnp.dot(
                 flux_in[step],
                 kbuf[c, half_cells : 2 * half_cells, :],
                 preferred_element_type=F32,
             )
-            for e in range(each):
-                zt[c * each + e] += got[:, e * LANES : (e + 1) * LANES]
-            return carry
-
-        lax.fori_loop(0, kbuf.shape[0], own_part, 0)
-        swap.wait()
-        lax.fori_loop(0, kbuf.shape[0], other_part, 0)
+            for c in range(columns)
+        ]
+        zt = [
+            spatial[t // each][:, t % each * LANES : (t % each + 1) * LANES]
+            for t in range(tiles)
+        ]
         parts = []
         for j in range(win_tiles):
             picked = jnp.zeros((rows, LANES), F32)
@@ -431,7 +428,6 @@
             pltpu.VMEM((2, rows, sounds), F32),
             pltpu.VMEM((2, rows, sounds), F32),
             pltpu.VMEM((half_cells // wide, 2 * half_cells, wide), BF16),
-            pltpu.VMEM((tiles, rows, LANES), F32),
             pltpu.VMEM((2, LANES, 2 * half_cells), F32),
             pltpu.SemaphoreType.DMA((len(arguments),)),
             pltpu.SemaphoreType.DMA((5,)),
@@ -440,7 +436,7 @@
             pltpu.SemaphoreType.DMA((5, n)),
         ],
         compiler_params=pltpu.CompilerParams(
-            collective_id=0, has_side_effects=True, vmem_limit_bytes=48 * 1024 * 1024
+            collective_id=0, has_side_effects=True, vmem_limit_bytes=60 * 1024 * 1024
         ),
     )(*arguments)
 

time: 51.4 us -> 47.9 us (0.932)
  local copies, waits for them, and re-layouts: 6.99 us -> 2.62 us
  Pallas kernels: 43.3 us -> 44.4 us
    unnamed x16 -> x2, local copies, waits for them, and re-layouts: 6.99 us -> 2.62 us
    pallas_call x1, Pallas kernels: 43.3 us -> 44.4 us  [body(): pl.pallas_call(functools.partial(kernel, n), out_shape=(jax.ShapeDtypeStr...]
where the time goes in v3:
time: 47.9 us; the launch traced here: 47.7 us
  Pallas kernels  44.4 us (93%)
  local copies, waits for them, and re-layouts  2.62 us (5%)
  between operations  0.64 us (1%)
    pallas_call x1, Pallas kernels, body(): pl.pallas_call(functools.partial(kernel, n), out_shape=(jax.ShapeDtypeStr...  44.4 us
    unnamed x2, local copies, waits for them, and re-layouts  2.62 us

profile of v3, /device:TPU:0, one launch (start us, length us, event | category | flops | bytes accessed | tf_op | source)
XLA Modules:
  0.0 47.7 jit_solution(57385388846671961)
XLA Ops:
  0.6 44.4 %shard_map.86 = (f32[4,4]{1,0:T(4,128)}, f32[8,4,256]{2,1,0:T(4,128)}) custom-call(f32[8,4,256]{2,1,0:T(4,128)} %probes_hbm.1, bf16[8,512,256]{2,1,0:T(8,128)(2,1)} %foot_hbm.1, f32[4,8]{1,0:T(4,128)} %bitcast.3, s32[4,8]{1,0:T(4,128)} %bitcast.4, s32[1,8]{1,0:T(1,128)} %bitcast.5, s32[2,3072]{1,0:T(2,128)} %coords_hbm.1, f32[16,16]{1,0:T(8,128)} %temporal_hbm.1), custom_call_target="tpu_custom_call" | custom-call | tf_op jit(solution)/shard_map/pallas_call | solution.py:412
  45.1 1.2 %copy.11 = f32[4,4]{1,0:T(4,128)} copy(f32[4,4]{1,0:T(4,128)} %get-tuple-element.4) | data formatting | bytes 128
  46.3 1.4 %copy.12 = f32[8,4,256]{2,1,0:T(4,128)} copy(f32[8,4,256]{2,1,0:T(4,128)} %get-tuple-element.5) | data formatting | bytes 65536

commit v4 on v3

--- a/solution.py
+++ b/solution.py
@@ -16,8 +16,8 @@
 F32 = jnp.float32
 BF16 = jnp.bfloat16
 LANES = 128
-first_tiles = 5
-early_tiles = 9
+early_chunks = 1
+depth = 16
 
 
 def kernel(
@@ -47,7 +47,8 @@
     image_out,
     image_in,
     kbuf,
-    features,
+    features_in,
+    features_out,
     fetch_sem,
     pair_send,
     pair_recv,
@@ -132,44 +133,14 @@
 
         lax.fori_loop(1, n, step, 0)
 
-    fetches[0].wait()
-    x, y = coords_ref[0:1, :], coords_ref[1:2, :]
-    square = x * x + y * y
-    upper = jnp.bitwise_and(square, -64)
-    ones = jnp.ones_like(x)
-    blank = jnp.zeros((LANES - 6, x.shape[1]), F32)
-
-    def feature_rows(parts):
-        return jnp.concatenate([part.astype(F32) for part in parts] + [blank], axis=0)
-
-    features[0] = feature_rows([x * -2, y * -2, upper, square - upper, ones, ones])
-    features[1] = feature_rows([x, y, ones, ones, upper, square - upper])
-    wide = kbuf.shape[2]
-    own_start = pl.multiple_of(half * half_cells, LANES)
-    rate = -math.log2(math.e) / kernel_length
-
-    def build(i, carry):
-        own = i < tiles
-        side = jnp.where(own, half, 1 - half)
-        start = side * half_cells + jnp.where(own, i, i - tiles) * LANES
-        left = jnp.transpose(features[0, :, pl.ds(pl.multiple_of(start, LANES), LANES)])
-        left = left.astype(BF16)
-        at = pl.multiple_of(i * LANES, LANES)
-        for c in range(kbuf.shape[0]):
-            right = features[
-                1, :, pl.ds(pl.multiple_of(own_start + c * wide, LANES), wide)
-            ].astype(BF16)
-            squared = jnp.dot(left, right, preferred_element_type=F32)
-            power = squared * rate * lax.rsqrt(jnp.maximum(squared, 0.5))
-            kbuf[c, pl.ds(at, LANES), :] = jnp.exp2(power).astype(BF16)
-        return carry
-
-    lax.fori_loop(0, first_tiles, build, 0)
-
-    for fetch in fetches[1:6]:
+    for fetch in fetches[0:6]:
         fetch.wait()
     for p in range(probes_n):
         pbuf[half, p * blocks : (p + 1) * blocks, :] = probes_ref[:, p, :]
+
+    pl.semaphore_wait(barrier, n)
+    send_probes = pair_copy(pbuf.at[half], pbuf.at[half], 0)
+    send_probes.start()
 
     span = meta.shape[2]
     lane = lax.broadcasted_iota(jnp.int32, (blocks, span), 1)
@@ -188,13 +159,42 @@
         weight = weight + jnp.where(chosen, upright(lag_ref[k : k + 1, :]), 0.0)
     tile_column = upright(tile_ref[0:1, :])
     meta[me] = jnp.where(lane == span - 1, tile_column, weight)
-
-    pl.semaphore_wait(barrier, n)
-    send_probes = pair_copy(pbuf.at[half], pbuf.at[half], 0)
-    send_probes.start()
     share(meta, 0)
 
-    lax.fori_loop(first_tiles, early_tiles, build, 0)
+    x, y = coords_ref[0:1, :], coords_ref[1:2, :]
+    square = x * x + y * y
+    upper = jnp.bitwise_and(square, -64)
+    ones = jnp.ones_like(x)
+    blank = jnp.zeros((depth - 6, x.shape[1]), F32)
+
+    def feature_rows(parts):
+        return jnp.concatenate([part.astype(F32) for part in parts] + [blank], axis=0)
+
+    features_in[...] = jnp.transpose(
+        feature_rows([x * -2, y * -2, upper, square - upper, ones, ones])
+    ).astype(BF16)
+    features_out[...] = feature_rows([x, y, ones, ones, upper, square - upper]).astype(BF16)
+    wide = kbuf.shape[2]
+    own_start = pl.multiple_of(half * half_cells, LANES)
+    rate = -math.log2(math.e) / kernel_length
+    chunk = max(size for size in (1, 2, 3, 4) if tiles % size == 0)
+    half_chunks = tiles // chunk
+    height = chunk * LANES
+
+    def build(i, carry):
+        own = i < half_chunks
+        side = jnp.where(own, half, 1 - half)
+        start = side * half_cells + jnp.where(own, i, i - half_chunks) * height
+        left = features_in[pl.ds(pl.multiple_of(start, height), height), :]
+        at = pl.multiple_of(i * height, height)
+        for c in range(kbuf.shape[0]):
+            right = features_out[:, pl.ds(pl.multiple_of(own_start + c * wide, LANES), wide)]
+            squared = jnp.dot(left, right, preferred_element_type=F32)
+            power = squared * rate * lax.rsqrt(jnp.maximum(squared, 0.5))
+            kbuf[c, pl.ds(at, height), :] = jnp.exp2(power.astype(BF16))
+        return carry
+
+    lax.fori_loop(0, early_chunks, build, 0)
 
     row_block = lax.rem(lax.broadcasted_iota(jnp.int32, (rows, LANES), 0), blocks)
 
@@ -330,7 +330,7 @@
     probe = jnp.concatenate([pbuf[0], pbuf[1]], axis=1)
     back(probe, 0)
 
-    lax.fori_loop(early_tiles, 2 * tiles, build, 0)
+    lax.fori_loop(early_chunks, 2 * half_chunks, build, 0)
 
     collect(meta, 0)
     weight_rows = meta[me, 0:blocks, 0:n]
@@ -409,13 +409,14 @@
         temporal,
     )
     vmem = pl.BlockSpec(memory_space=pltpu.VMEM)
+    hbm = pl.BlockSpec(memory_space=pltpu.HBM)
     return pl.pallas_call(
         functools.partial(kernel, n),
         out_shape=(
             jax.ShapeDtypeStruct((4, probes_n), F32),
             jax.ShapeDtypeStruct(probes.shape, F32),
         ),
-        in_specs=[pl.BlockSpec(memory_space=pltpu.HBM)] * len(arguments),
+        in_specs=[hbm] * len(arguments),
         out_specs=(vmem, vmem),
         scratch_shapes=[
             *[pltpu.VMEM(argument.shape, argument.dtype) for argument in arguments],
@@ -428,7 +429,8 @@
             pltpu.VMEM((2, rows, sounds), F32),
             pltpu.VMEM((2, rows, sounds), F32),
             pltpu.VMEM((half_cells // wide, 2 * half_cells, wide), BF16),
-            pltpu.VMEM((2, LANES, 2 * half_cells), F32),
+            pltpu.VMEM((2 * half_cells, depth), BF16),
+            pltpu.VMEM((depth, 2 * half_cells), BF16),
             pltpu.SemaphoreType.DMA((len(arguments),)),
             pltpu.SemaphoreType.DMA((5,)),
             pltpu.SemaphoreType.DMA((5,)),

time: 47.9 us -> 46.6 us (0.973)
  Pallas kernels: 44.4 us -> 43.1 us
    pallas_call x1, Pallas kernels: 44.4 us -> 43.1 us  [body(): pl.pallas_call(functools.partial(kernel, n), out_shape=(jax.ShapeDtypeStr...]
where the time goes in v4:
time: 46.6 us; the launch traced here: 46.4 us
  Pallas kernels  43.1 us (92%)
  local copies, waits for them, and re-layouts  2.62 us (6%)
  between operations  0.64 us (1%)
    pallas_call x1, Pallas kernels, body(): pl.pallas_call(functools.partial(kernel, n), out_shape=(jax.ShapeDtypeStr...  43.1 us
    unnamed x2, local copies, waits for them, and re-layouts  2.62 us

profile of v4, /device:TPU:0, one launch (start us, length us, event | category | flops | bytes accessed | tf_op | source)
XLA Modules:
  0.0 46.4 jit_solution(6831910727452056883)
XLA Ops:
  0.6 43.1 %shard_map.86 = (f32[4,4]{1,0:T(4,128)}, f32[8,4,256]{2,1,0:T(4,128)}) custom-call(f32[8,4,256]{2,1,0:T(4,128)} %probes_hbm.1, bf16[8,512,256]{2,1,0:T(8,128)(2,1)} %foot_hbm.1, f32[4,8]{1,0:T(4,128)} %bitcast.3, s32[4,8]{1,0:T(4,128)} %bitcast.4, s32[1,8]{1,0:T(1,128)} %bitcast.5, s32[2,3072]{1,0:T(2,128)} %coords_hbm.1, f32[16,16]{1,0:T(8,128)} %temporal_hbm.1), custom_call_target="tpu_custom_call" | custom-call | tf_op jit(solution)/shard_map/pallas_call | solution.py:413
  43.8 1.2 %copy.11 = f32[4,4]{1,0:T(4,128)} copy(f32[4,4]{1,0:T(4,128)} %get-tuple-element.4) | data formatting | bytes 128
  45.0 1.4 %copy.12 = f32[8,4,256]{2,1,0:T(4,128)} copy(f32[8,4,256]{2,1,0:T(4,128)} %get-tuple-element.5) | data formatting | bytes 65536

commit v5 on v4

--- a/solution.py
+++ b/solution.py
@@ -117,7 +117,7 @@
             peer_copy(slots, me, which, k).start()
             return carry
 
-        lax.fori_loop(1, n, step, 0)
+        lax.fori_loop(1, n, step, 0, unroll=5 if n % 5 == 1 else 1)
 
     def collect(slots, which):
         def step(k, carry):

time: 46.6 us -> 46.6 us (level)
  no operation moved by 1% of the time
where the time goes in v5:
time: 46.6 us; the launch traced here: 46.4 us
  Pallas kernels  43.1 us (92%)
  local copies, waits for them, and re-layouts  2.62 us (6%)
  between operations  0.64 us (1%)
    pallas_call x1, Pallas kernels, body(): pl.pallas_call(functools.partial(kernel, n), out_shape=(jax.ShapeDtypeStr...  43.1 us
    unnamed x2, local copies, waits for them, and re-layouts  2.62 us

profile of v5, /device:TPU:0, one launch (start us, length us, event | category | flops | bytes accessed | tf_op | source)
XLA Modules:
  0.0 46.4 jit_solution(721092164706485269)
XLA Ops:
  0.6 43.1 %shard_map.86 = (f32[4,4]{1,0:T(4,128)}, f32[8,4,256]{2,1,0:T(4,128)}) custom-call(f32[8,4,256]{2,1,0:T(4,128)} %probes_hbm.1, bf16[8,512,256]{2,1,0:T(8,128)(2,1)} %foot_hbm.1, f32[4,8]{1,0:T(4,128)} %bitcast.3, s32[4,8]{1,0:T(4,128)} %bitcast.4, s32[1,8]{1,0:T(1,128)} %bitcast.5, s32[2,3072]{1,0:T(2,128)} %coords_hbm.1, f32[16,16]{1,0:T(8,128)} %temporal_hbm.1), custom_call_target="tpu_custom_call" | custom-call | tf_op jit(solution)/shard_map/pallas_call | solution.py:413
  43.7 1.2 %copy.11 = f32[4,4]{1,0:T(4,128)} copy(f32[4,4]{1,0:T(4,128)} %get-tuple-element.4) | data formatting | bytes 128
  45.0 1.4 %copy.12 = f32[8,4,256]{2,1,0:T(4,128)} copy(f32[8,4,256]{2,1,0:T(4,128)} %get-tuple-element.5) | data formatting | bytes 65536
